TPU v7x, 32 devices: a whole 2x2x4 slice. The times are simulated.
32 devices in a mesh: ia: 8 (over z, x), ja: 2 (over y), row: 2 (over core).
Axes of the slice: x: 2, y: 2, z: 4, core: 2. Of those that a mesh axis runs over, the one named last changes fastest.
Arguments:
- amplitudes: float32 [16, 16, 1024, 1024], P('ia', ('ja', 'row')), may hold values from -6 to 6
- cycle_inter: float32 [2, 16, 1024, 1024], P(None, ('ja', 'row'), 'ia'), may hold values from -0.125 to 0.125
- occ_energy: float32 [256], replicated, may hold values from -2 to -0.3
- virt_energy: float32 [1024], replicated, may hold values from 0.3 to 3
- window_orbs: int32 [16], replicated, may hold values from 0 to 255, as said below
- internal_pos: int32 [2], replicated, may hold values from 0 to 15, as said below
- virt_order: int32 [1024], replicated, may hold values from 0 to 1023, each once
Outputs:
- updated: float32 [16, 16, 1024, 1024], P('ia', ('ja', 'row'))
Inputs may be any that keep to these rules, and one draw needn't show every extreme that they name: `window_orbs`: 16 distinct orbital numbers. `internal_pos`: 2 distinct window positions, one of which is the last position 15.
All inputs are finite; a program needn't handle non-finite values.
Results may differ from a plain program's by a relative error of at most 0.00005.
Values sent between devices are 32-bit elements; how exact they have to be, the bound alone decides.
A program may use at most 192 MiB of HBM per device.

v0:
```python
import jax
import jax.numpy as jnp
from jax import lax
from jax.sharding import PartitionSpec as P


def spread(array, axis, root):
    mine = lax.axis_index(axis) == root
    return lax.psum(jnp.where(mine, array, jnp.zeros_like(array)), axis)


def on_device(
    amplitudes, cycle_inter, occ_energy, virt_energy, window_orbs, internal_pos, virt_order
):
    tile_rows = amplitudes.shape[0]
    tile_cols = amplitudes.shape[1]
    count_k = cycle_inter.shape[0]
    formed = []
    for which in range(count_k):
        target = internal_pos[which]
        local_col = target % tile_cols
        owner = target // tile_cols
        picked = lax.dynamic_index_in_dim(amplitudes, local_col, 1, keepdims=False)
        doubled = 2.0 * picked - jnp.swapaxes(picked, 1, 2)
        formed.append(spread(doubled, ("ja", "row"), owner))
    pair_x = jnp.stack(formed, axis=0)
    cycle = jnp.einsum(
        "kiac,kjcb->ijab",
        pair_x,
        lax.all_gather(cycle_inter, "ia", axis=2, tiled=True),
        precision=lax.Precision.HIGHEST,
        preferred_element_type=jnp.float32,
    )
    first_leg = lax.all_to_all(cycle, ("ja", "row"), split_axis=2, concat_axis=1, tiled=True)
    second_leg = lax.all_to_all(first_leg, "ia", split_axis=1, concat_axis=0, tiled=True)
    arrived = lax.all_to_all(second_leg, ("ja", "row"), split_axis=0, concat_axis=2, tiled=True)
    mirrored = jnp.transpose(arrived, (1, 0, 3, 2))
    hits = window_orbs[:, None] == jnp.arange(occ_energy.shape[0], dtype=jnp.int32)[None, :]
    e_window = jnp.sum(jnp.where(hits, occ_energy[None, :], 0.0), axis=1)
    e_virt = jnp.take(virt_energy, virt_order)
    e_rows = lax.dynamic_slice_in_dim(e_window, lax.axis_index("ia") * tile_rows, tile_rows)
    e_cols = lax.dynamic_slice_in_dim(
        e_window, lax.axis_index(("ja", "row")) * tile_cols, tile_cols
    )
    denom = (
        e_rows[:, None, None, None]
        + e_cols[None, :, None, None]
        - e_virt[None, None, :, None]
        - e_virt[None, None, None, :]
    )
    return amplitudes + (cycle + mirrored) / denom


def solution(mesh):
    placed = (
        P("ia", ("ja", "row"), None, None),
        P(None, ("ja", "row"), "ia", None),
        P(),
        P(),
        P(),
        P(),
        P(),
    )
    return jax.shard_map(
        on_device,
        mesh=mesh,
        in_specs=placed,
        out_specs=P("ia", ("ja", "row"), None, None),
        check_vma=False,
    )
```

profile of v0, /device:TPU:0, one launch (start us, length us, event | category | flops | bytes accessed | tf_op | source)
XLA Modules:
  0.0 2673.2 jit_solution(12715529252360509927)
XLA Ops:
  13.9 11.0 constant_dynamic-slice_fusion
  24.9 8.7 copy.45
  33.6 8.7 bitcast_multiply_fusion
  42.3 8.7 copy.46
  51.0 8.7 copy.47
  59.6 12.2 bitcast_subtract_fusion
  71.9 8.7 copy.48
  80.5 12.0 fusion.10
  102.7 288.8 %all-reduce.3.cloned.1.call-done = (f32[1,2,1024,1024]{3,2,0,1:T(8,128)}, f32[1,2,1024,1024]{3,2,1,0:T(8,128)}) async-done(((f32[1,2,1024,1024]{3,2,0,1:T(8,128)}, f32[1,2,1024,1024]{3,2,1,0:T(8,128)}), (f32[1,2,1024,1024]{3,2,0,1:T(8,128)}, f32[1,2,1024,1024]{3,2,1,0:T(8,128)})) %all-reduce.3.cloned.1.call-update) | async-done | bytes 16777232 | tf_op jit(solution)/shard_map/psum | solution.py:9
  391.5 11.9 maximum_bitcast_fusion.4
  403.5 341.6 %all-gather.2.cloned.1.call-done = f32[2,4,1024,1024]{3,2,0,1:T(8,128)} async-done(((f32[2,4,128,1024]{3,2,0,1:T(8,128)}), f32[2,4,1024,1024]{3,2,0,1:T(8,128)}) %all-gather.2.cloned.1.call-update) | async-done | bytes 33554448 | tf_op jit(solution)/shard_map/all_gather | solution.py:30
  745.1 221.3 %fusion.4 = f32[2,4,1024,1024]{3,2,1,0:T(8,128)} fusion(f32[2,4,1024,1024]{3,2,0,1:T(8,128)} %all-gather.2.cloned.1.call-done, f32[2,2,1024,1024,1]{3,2,0,4,1:T(8,128)} %maximum_bitcast_fusion.4), kind=kOutput, calls=%fused_computation.6 | convolution fusion | flops 206158430208 | bytes 83886080 | tf_op jit(solution)/shard_map/kiac,kjcb->ijab/dot_general | solution.py:27
  966.4 37.9 %copy.51 = f32[2,4,1024,1024]{3,1,0,2:T(4,128)} copy(f32[2,4,1024,1024]{3,2,1,0:T(8,128)} %fusion.4) | data formatting | bytes 67108864 | tf_op jit(solution)/shard_map/kiac,kjcb->ijab/transpose | solution.py:27
  1004.3 368.7 %all_to_all.54 = f32[2,4,1024,1024]{3,1,0,2:T(4,128)S(1)} all-to-all(f32[2,4,1024,1024]{3,1,0,2:T(4,128)} %copy.51), channel_id=1, replica_groups=mesh['ia'=8,'ja'=2,'row'=2] {'ja','row'}, dimensions={2} | all-to-all | bytes 67108864 | tf_op jit(solution)/shard_map/all_to_all | solution.py:34
  1373.0 37.0 %copy.52 = f32[2,4,1024,1024]{3,2,1,0:T(8,128)} copy(f32[2,4,1024,1024]{3,1,0,2:T(4,128)S(1)} %all_to_all.54) | data formatting | bytes 67108864 | tf_op jit(solution)/shard_map/all_to_all | solution.py:34
  1410.0 12.1 copy.53
  1422.1 11.1 copy.54
  1433.1 727.0 %all_to_all.55 = f32[2,16,256,1024]{3,2,0,1:T(8,128)S(1)} all-to-all(f32[2,16,256,1024]{3,2,0,1:T(8,128)} %copy.54), channel_id=1, replica_groups=mesh['ia'=8,'ja'=2,'row'=2] {'ia'}, dimensions={1} | all-to-all | bytes 67108864 | tf_op jit(solution)/shard_map/all_to_all | solution.py:35
  2160.2 11.0 copy.56
  2171.2 9.8 all-to-all-start.2
  2186.1 357.8 %all-to-all-done.2 = f32[16,2,256,1024]{3,2,1,0:T(8,128)} async-done(((f32[16,2,256,1024]{3,2,1,0:T(8,128)}), f32[16,2,256,1024]{3,2,1,0:T(8,128)}, u32[]{:S(2)}, u32[]{:S(2)}) %all-to-all-start.2) | async-done | bytes 33554464 | tf_op jit(solution)/shard_map/all_to_all | solution.py:36
  2543.9 38.2 %copy.57 = f32[4,2,4,256,1024]{3,2,4,0,1:T(4,128)} copy(f32[4,2,4,256,1024]{4,3,1,0,2:T(8,128)} %bitcast.24) | data formatting | bytes 67108864 | tf_op jit(solution)/shard_map/all_to_all | solution.py:36
  2582.1 40.5 %all_to_all.50 = f32[4,2,1024,1024]{2,3,0,1:T(8,128)} reshape(f32[4,2,4,256,1024]{3,2,4,0,1:T(4,128)} %copy.57) | data formatting | bytes 67108864 | tf_op jit(solution)/shard_map/all_to_all | solution.py:36
  2622.6 43.2 %fusion.1 = f32[2,4,1024,1024]{3,2,1,0:T(8,128)} fusion(f32[2,4,1024,1024]{3,2,1,0:T(8,128)} %param.7, f32[2,4,1024,1024]{3,2,1,0:T(8,128)} %fusion.4, f32[4,2,1024,1024]{2,3,0,1:T(8,128)} %all_to_all.50, f32[1024]{0:T(1024)S(1)} %and_select_fusion, f32[2,4,1024]{2,1,0:T(4,128)S(1)} %broadcast_subtract_fusion), kind=kLoop, calls=%fused_computation.3 | loop fusion | flops 33554432 | bytes 134254592 | tf_op jit(solution)/shard_map/add | solution.py:51
  (23 shorter events, 16.5 us)
Async XLA Ops:
  7.4 2174.1 %copy-start = (f32[1024]{0:T(1024)S(1)}, f32[1024]{0:T(1024)}, u32[]{:S(2)}) copy-start(f32[1024]{0:T(1024)} %param.10) | copy-start | bytes 12292
  7.4 384.1 %all-reduce.3.cloned.1.call-start = ((), (), s32[]{:S(2)}) async-start(), calls=%async_computation.4 | async-start | bytes 33554432 | tf_op jit(solution)/shard_map/psum | solution.py:9
  97.9 647.2 %all-gather.2.cloned.1.call-start = ((), (), s32[]{:S(2)}) async-start(), calls=%async_computation.3 | async-start | bytes 37748736 | tf_op jit(solution)/shard_map/all_gather | solution.py:30
  2171.2 9.9 copy-start.2
  2171.2 9.9 copy-start.3
  2171.2 10.2 copy-start.1
  2171.2 372.7 %all-to-all-start.2 = ((f32[16,2,256,1024]{3,2,1,0:T(8,128)}), f32[16,2,256,1024]{3,2,1,0:T(8,128)}, u32[]{:S(2)}, u32[]{:S(2)}) async-start(f32[16,2,256,1024]{3,2,1,0:T(8,128)} %bitcast.61), calls=%async_computation.2 | async-start | bytes 67108864 | tf_op jit(solution)/shard_map/all_to_all | solution.py:36
Sparse Core Ops, SparseCore 0:
  98.0 293.4 all-reduce.2
Sparse Core Ops, SparseCore 1:
  102.8 642.2 all-gather.1
where the time goes:
time: 2680 us; the launch traced here: 2670 us
  blocking collectives  1100 us (41%)
  waiting for transfers between devices  988 us (37%)
  local copies, waits for them, and re-layouts  244 us (9%)
  matrix products  221 us (8%)
  other arithmetic  93.7 us (3%)
    all_to_all x1, blocking collectives, on_device(): lax.all_to_all(first_leg, 'ia', split_axis=1, concat_axis=0, tiled=True)  727 us
    all_to_all x1, blocking collectives, on_device(): lax.all_to_all(cycle, ('ja', 'row'), split_axis=2, concat_axis=1, tiled=T...  369 us
    all_to_all x1, waiting for transfers between devices, on_device(): lax.all_to_all(second_leg, ('ja', 'row'), split_axis=0, concat_axis=2, ti...  358 us
    all_gather x1, waiting for transfers between devices, on_device(): lax.all_gather(cycle_inter, 'ia', axis=2, tiled=True)  342 us
    psum x1, waiting for transfers between devices, spread(): return lax.psum(jnp.where(mine, array, jnp.zeros_like(array)), axis)  289 us
    dot_general x1, matrix products, on_device(): jnp.einsum('kiac,kjcb->ijab', pair_x, lax.all_gather(cycle_inter, 'ia', a...  221 us
    all_to_all x2, local copies, waits for them, and re-layouts, on_device(): lax.all_to_all(second_leg, ('ja', 'row'), split_axis=0, concat_axis=2, ti...  78.7 us
    all_to_all x3, local copies, waits for them, and re-layouts, on_device(): lax.all_to_all(cycle, ('ja', 'row'), split_axis=2, concat_axis=1, tiled=T...  60.1 us
  transfers between devices with their start and end apart: 3, of which 3 were waited for; matrix products, arithmetic and copies ran while one was open for 1% of the time, Pallas kernels for 0%

commit v1 on v0

v1 whole, which is shorter than its diff:
```python
import functools

import jax
import jax.numpy as jnp
from jax import lax
from jax.experimental import pallas as pl
from jax.experimental.pallas import tpu as pltpu
from jax.sharding import PartitionSpec as P

COLS = ("ja", "row")
ALL = ("ia", "ja", "row")


def mirror(blocks_for, ia_size, jr_size):
    k = ia_size // jr_size
    sub = lax.rem(lax.axis_index("ia"), k)
    got = []
    for turn in range(k):
        pairs = []
        for a in range(jr_size):
            for s in range(k):
                for b in range(jr_size):
                    t = (turn - s) % k
                    pairs.append(((k * a + s) * jr_size + b, (k * b + t) * jr_size + a))
        other = lax.rem(turn - sub + k, k)
        got.append((other, lax.ppermute(blocks_for(other), ALL, pairs)))
    return got


def ring_gather(piece, ia_size, depth):
    lead = piece.shape[:2]
    width = piece.shape[3]
    me = lax.axis_index("ia")
    swap = [(d, d ^ 1) for d in range(ia_size)]
    step = [(d, (d + 2) % ia_size) for d in range(ia_size)]
    full = jnp.zeros(lead + (ia_size * depth, width), piece.dtype)
    marks = []
    for s in range(ia_size // 2):
        owner = lax.rem(me - 2 * s + ia_size, ia_size)
        partner = lax.ppermute(piece, "ia", swap)
        marks.append(partner)
        following = lax.ppermute(piece, "ia", step) if s < ia_size // 2 - 1 else None
        full = lax.dynamic_update_slice_in_dim(full, piece, owner * depth, 2)
        full = lax.dynamic_update_slice_in_dim(full, partner, (owner ^ 1) * depth, 2)
        piece = following
    return full, marks


def split(value):
    high = value.astype(jnp.bfloat16)
    return high, (value - high.astype(jnp.float32)).astype(jnp.bfloat16)


def form_rows(amplitudes, internal_pos):
    tile_rows, tile_cols, virt, _ = amplitudes.shape
    count_k = internal_pos.shape[0]
    band = 256 if virt % 256 == 0 else virt

    def body(at_col, where, local, amp_ref, out_ref):
        mine = where[pl.program_id(0)] == at_col[0]
        for at in range(virt // band):
            rows = slice(at * band, (at + 1) * band)
            formed = 2.0 * amp_ref[0, 0, rows, :] - amp_ref[0, 0, :, rows].T
            out_ref[0, 0, rows, :] = jnp.where(mine, formed, 0.0)

    return pl.pallas_call(
        body,
        grid_spec=pltpu.PrefetchScalarGridSpec(
            num_scalar_prefetch=3,
            grid=(count_k, tile_rows),
            in_specs=[
                pl.BlockSpec((1, 1, virt, virt), lambda m, i, c, w, local: (i, local[m], 0, 0))
            ],
            out_specs=pl.BlockSpec((1, 1, virt, virt), lambda m, i, c, w, local: (m, i, 0, 0)),
        ),
        out_shape=jax.ShapeDtypeStruct((count_k, tile_rows, virt, virt), jnp.float32),
        compiler_params=pltpu.CompilerParams(vmem_limit_bytes=40 * 1024 * 1024),
        name="form_rows",
    )(
        lax.axis_index(COLS).astype(jnp.int32)[None],
        internal_pos // tile_cols,
        internal_pos % tile_cols,
        amplitudes,
    )


def turned(x_rows, which, depth):
    count_k, tile_rows, virt, _ = x_rows.shape
    if depth % 128:
        block = lax.dynamic_slice_in_dim(x_rows, which * depth, depth, 3)
        return jnp.swapaxes(block, 2, 3)

    def body(at, x_ref, out_ref):
        out_ref[0, 0] = x_ref[0, 0].T

    return pl.pallas_call(
        body,
        grid_spec=pltpu.PrefetchScalarGridSpec(
            num_scalar_prefetch=1,
            grid=(count_k, tile_rows),
            in_specs=[pl.BlockSpec((1, 1, virt, depth), lambda m, i, at: (m, i, 0, at[0]))],
            out_specs=pl.BlockSpec((1, 1, depth, virt), lambda m, i, at: (m, i, 0, 0)),
        ),
        out_shape=jax.ShapeDtypeStruct((count_k, tile_rows, depth, virt), jnp.float32),
        compiler_params=pltpu.CompilerParams(vmem_limit_bytes=52 * 1024 * 1024),
        name="turned",
    )(which.astype(jnp.int32)[None], x_rows)


def product_kernel(col, band, last, left_ref, right_ref, *rest):
    out_ref, total, high, low = rest[-4:]
    row, block = pl.program_id(0), pl.program_id(1)
    count_k, depth = right_ref.shape[0], right_ref.shape[2]
    for m in range(count_k):
        rows = pl.ds(m * depth, depth)
        high[rows, :], low[rows, :] = split(right_ref[m, 0])

    @pl.when(block == 0)
    def _():
        total[...] = jnp.zeros_like(total)

    def one_band(at, carry):
        rows = pl.ds(pl.multiple_of(at * band, band), band)
        left = jnp.concatenate([left_ref[m, 0, rows, :] for m in range(count_k)], axis=1)
        left_high, left_low = split(left)
        dot = functools.partial(jnp.dot, preferred_element_type=jnp.float32)
        total[rows, :] += (
            dot(left_high, high[...]) + dot(left_high, low[...]) + dot(left_low, high[...])
        )
        return carry

    bands = total.shape[0] // band
    lax.fori_loop(0, bands, one_band, 0)

    @pl.when(block == pl.num_programs(1) - 1)
    def _():
        if not last:
            out_ref[0, 0] = total[...]
            return
        held_ref, e_rows, e_cols, amp_ref, va_ref, vb_ref = rest[:6]
        pair = e_rows[row] + e_cols[col]

        def finish(at, carry):
            rows = pl.ds(pl.multiple_of(at * band, band), band)
            denom = (pair - va_ref[rows, :]) - vb_ref[...]
            both = held_ref[0, 0, rows, :] + total[rows, :]
            out_ref[0, 0, rows, :] = amp_ref[0, 0, rows, :] + both / denom
            return carry

        lax.fori_loop(0, bands, finish, 0)


def product(col, at, left, right, out, shape, energies=None):
    count_k, tile_rows, virt, _ = left.shape
    depth = 256 if virt % 256 == 0 else virt
    band = 256 if virt % 256 == 0 else virt
    tile = pl.BlockSpec((1, 1, virt, virt), lambda i, q: (i, col, 0, 0))
    in_specs = [
        pl.BlockSpec((count_k, 1, virt, depth), lambda i, q: (0, i, 0, q)),
        pl.BlockSpec((count_k, 1, depth, virt), lambda i, q: (0, at, q, 0)),
    ]
    operands = [left, right]
    aliases = {}
    if out is not None:
        aliases = {2: 0}
        in_specs.append(pl.BlockSpec(memory_space=pl.ANY) if energies is None else tile)
        operands.append(out)
    if energies is not None:
        e_rows, e_cols, amplitudes, e_virt = energies
        scalars = pl.BlockSpec(memory_space=pltpu.SMEM)
        in_specs += [
            scalars, scalars, tile,
            pl.BlockSpec((virt, 1), lambda i, q: (0, 0)),
            pl.BlockSpec((1, virt), lambda i, q: (0, 0)),
        ]
        operands += [e_rows, e_cols, amplitudes, e_virt[:, None], e_virt[None]]
    return pl.pallas_call(
        functools.partial(product_kernel, col, band, energies is not None),
        grid=(tile_rows, virt // depth),
        in_specs=in_specs,
        out_specs=tile,
        out_shape=jax.ShapeDtypeStruct(shape, jnp.float32),
        scratch_shapes=[
            pltpu.VMEM((virt, virt), jnp.float32),
            pltpu.VMEM((count_k * depth, virt), jnp.bfloat16),
            pltpu.VMEM((count_k * depth, virt), jnp.bfloat16),
        ],
        input_output_aliases=aliases,
        compiler_params=pltpu.CompilerParams(vmem_limit_bytes=52 * 1024 * 1024),
        cost_estimate=pl.CostEstimate(
            flops=6 * tile_rows * count_k * virt**3,
            bytes_accessed=10 * tile_rows * virt * virt * 4,
            transcendentals=0,
        ),
        name="product" if energies is None else "finish",
    )(*operands)


def on_device(
    amplitudes, cycle_inter, occ_energy, virt_energy, window_orbs, internal_pos, virt_order
):
    tile_rows, tile_cols = amplitudes.shape[:2]
    virt = amplitudes.shape[2]
    count_k = cycle_inter.shape[0]
    depth = cycle_inter.shape[2]
    ia_size = lax.axis_size("ia")
    jr_size = lax.axis_size("ja") * lax.axis_size("row")
    at_col = lax.axis_index(COLS)
    parts = 2 if tile_cols % 2 == 0 else 1
    share = tile_cols // parts

    w_cols, marks = [], []
    for h in range(parts):
        full, partners = ring_gather(cycle_inter[:, h * share : (h + 1) * share], ia_size, depth)
        w_cols.append(full)
        marks.append(partners[max(len(partners) - 2, 0)])

    k = ia_size // jr_size
    w_blocks = mirror(
        lambda t: lax.dynamic_slice_in_dim(cycle_inter, t * tile_rows, tile_rows, 1),
        ia_size,
        jr_size,
    )

    x_rows = lax.psum(form_rows(amplitudes, internal_pos), COLS)
    after = sum(jnp.isnan(mark[0, 0, 0, 0]).astype(jnp.int32) for mark in marks)

    chunk = jnp.zeros((count_k, tile_cols, depth, virt), jnp.float32)
    for s, block in mirror(
        lambda t: turned(x_rows, at_col * k + t + after, depth),
        ia_size,
        jr_size,
    ):
        chunk = lax.dynamic_update_slice_in_dim(chunk, block, s * tile_rows, 1)
    hits = window_orbs[:, None] == jnp.arange(occ_energy.shape[0], dtype=jnp.int32)[None, :]
    e_window = jnp.sum(jnp.where(hits, occ_energy[None, :], 0.0), axis=1)
    e_virt = jnp.take(virt_energy, virt_order)
    e_rows = lax.dynamic_slice_in_dim(e_window, lax.axis_index("ia") * tile_rows, tile_rows)
    e_cols = lax.dynamic_slice_in_dim(e_window, at_col * tile_cols, tile_cols)
    out = None
    for col in range(tile_cols):
        out = product(col, col % share, x_rows, w_cols[col // share], out, amplitudes.shape)
    energies = (e_rows, e_cols, amplitudes, e_virt)
    done = jnp.isnan(out[0, 0, 0, 0]).astype(jnp.int32)
    quarter = jnp.zeros((count_k, tile_rows, k * depth, virt), jnp.float32)
    for s, block in w_blocks:
        quarter = lax.dynamic_update_slice_in_dim(quarter, block, s * depth + done, 2)
    wt_rows = jnp.swapaxes(lax.all_gather(quarter, COLS, axis=2, tiled=True), 2, 3)
    for h in range(parts):
        piece = lax.dynamic_slice_in_dim(chunk, h * share + (done if h else 0), share, 1)
        x_cols = ring_gather(piece, ia_size, depth)[0]
        for at in range(share):
            out = product(h * share + at, at, wt_rows, x_cols, out, amplitudes.shape, energies)
    return out


def solution(mesh):
    placed = (
        P("ia", COLS, None, None),
        P(None, COLS, "ia", None),
        P(),
        P(),
        P(),
        P(),
        P(),
    )
    return jax.shard_map(
        on_device,
        mesh=mesh,
        in_specs=placed,
        out_specs=P("ia", COLS, None, None),
        check_vma=False,
    )
```

time: 2680 us -> 1510 us (0.56)
  blocking collectives: 1100 us -> 0 us
  waiting for transfers between devices: 988 us -> 608 us
  Pallas kernels: 0 us -> 358 us
  starting transfers between devices: 9.9 us -> 360 us
  matrix products: 221 us -> 0 us
  other arithmetic: 93.7 us -> 0.2 us
  local copies, waits for them, and re-layouts: 244 us -> 164 us
    all_to_all x2 -> x0, blocking collectives: 1100 us -> none  [the longest x1 727 us: on_device(): lax.all_to_all(first_leg, 'ia', split_axis=1, concat_axis=0, tiled=True)]
    ppermute x0 -> x32, waiting for transfers between devices: none -> 608 us  [the longest x16 338 us: ring_gather(): partner = lax.ppermute(piece, 'ia', swap)]
    ppermute x0 -> x32, starting transfers between devices: none -> 360 us  [the longest x12 317 us: ring_gather(): lax.ppermute(piece, 'ia', step)]
    all_to_all x1 -> x0, waiting for transfers between devices: 358 us -> none  [on_device(): lax.all_to_all(second_leg, ('ja', 'row'), split_axis=0, concat_axis=2, ti...]
    pallas_call x0 -> x11, Pallas kernels: none -> 358 us  [the longest x8 336 us: product(): pl.pallas_call(functools.partial(product_kernel, col, band, energies is n...]
    all_gather x1, waiting for transfers between devices: 342 us -> 0.01 us  [on_device(): lax.all_gather(quarter, COLS, axis=2, tiled=True)]
    psum x1, waiting for transfers between devices: 289 us -> 0.01 us  [on_device(): x_rows = lax.psum(form_rows(amplitudes, internal_pos), COLS)]
    dot_general x1 -> x0, matrix products: 221 us -> none  [on_device(): jnp.einsum('kiac,kjcb->ijab', pair_x, lax.all_gather(cycle_inter, 'ia', a...]
  transfers between devices with their start and end apart: 3 -> 34, of which waited for: 3 -> 20; matrix products, arithmetic and copies ran while one was open for 1% -> 9% of each run, Pallas kernels for 0% -> 12%
where the time goes in v1:
time: 1510 us
  waiting for transfers between devices  608 us (40%)
  starting transfers between devices  360 us (24%)
  Pallas kernels  358 us (24%)
  local copies, waits for them, and re-layouts  164 us (11%)
  between operations  17.4 us (1%)
    ppermute x16, waiting for transfers between devices, ring_gather(): partner = lax.ppermute(piece, 'ia', swap)  338 us
    pallas_call x8, Pallas kernels, product(): pl.pallas_call(functools.partial(product_kernel, col, band, energies is n...  336 us
    ppermute x12, starting transfers between devices, ring_gather(): lax.ppermute(piece, 'ia', step)  317 us
    ppermute x12, waiting for transfers between devices, ring_gather(): lax.ppermute(piece, 'ia', step)  227 us
    dynamic_update_slice x16, local copies, waits for them, and re-layouts, ring_gather(): lax.dynamic_update_slice_in_dim(full, partner, (owner ^ 1) * depth, 2)  45.4 us
    ppermute x4, waiting for transfers between devices, mirror(): got.append((other, lax.ppermute(blocks_for(other), ALL, pairs)))  43 us
    dynamic_update_slice x14, local copies, waits for them, and re-layouts, ring_gather(): full = lax.dynamic_update_slice_in_dim(full, piece, owner * depth, 2)  39.4 us
    another operation x4, local copies, waits for them, and re-layouts  31.6 us
  transfers between devices with their start and end apart: 34, of which 20 were waited for; matrix products, arithmetic and copies ran while one was open for 9% of the time, Pallas kernels for 12%

profile of v1, /device:TPU:0, one launch (start us, length us, event | category | flops | bytes accessed | tf_op | source)
XLA Modules:
  0.0 1507.3 jit_solution(3229209306791673360)
XLA Ops:
  72.6 43.1 %collective-permute-done.2 = f32[2,2,128,1024]{3,2,1,0:T(8,128)S(1)} collective-permute-done((f32[2,2,128,1024]{3,2,1,0:T(8,128)}, f32[2,2,128,1024]{3,2,1,0:T(8,128)S(1)}, u32[]{:S(2)}, u32[]{:S(2)}) %collective-permute-start.2) | collective-permute-done | bytes 2097184 | tf_op jit(solution)/shard_map/ppermute | solution.py:42
  118.7 42.0 %collective-permute-done.11 = f32[2,2,128,1024]{3,2,1,0:T(8,128)} collective-permute-done((f32[2,2,128,1024]{3,2,1,0:T(8,128)}, f32[2,2,128,1024]{3,2,1,0:T(8,128)}, u32[]{:S(2)}, u32[]{:S(2)}) %collective-permute-start.11) | collective-permute-done | bytes 2097184 | tf_op jit(solution)/shard_map/ppermute | solution.py:42
  162.5 43.1 %collective-permute-done.4 = f32[2,2,128,1024]{3,2,1,0:T(8,128)} collective-permute-done((f32[2,2,128,1024]{3,2,1,0:T(8,128)S(1)}, f32[2,2,128,1024]{3,2,1,0:T(8,128)}, u32[]{:S(2)}, u32[]{:S(2)}) %collective-permute-start.4) | collective-permute-done | bytes 2097184 | tf_op jit(solution)/shard_map/ppermute | solution.py:42
  211.1 39.5 %collective-permute-done.13 = f32[2,2,128,1024]{3,2,1,0:T(8,128)} collective-permute-done((f32[2,2,128,1024]{3,2,1,0:T(8,128)}, f32[2,2,128,1024]{3,2,1,0:T(8,128)}, u32[]{:S(2)}, u32[]{:S(2)}) %collective-permute-start.13) | collective-permute-done | bytes 2097184 | tf_op jit(solution)/shard_map/ppermute | solution.py:42
  316.0 73.3 %collective-permute-done.12 = f32[2,2,128,1024]{3,2,1,0:T(8,128)} collective-permute-done((f32[2,2,128,1024]{3,2,1,0:T(8,128)}, f32[2,2,128,1024]{3,2,1,0:T(8,128)}, u32[]{:S(2)}, u32[]{:S(2)}) %collective-permute-start.12) | collective-permute-done | bytes 2097184 | tf_op jit(solution)/shard_map/ppermute | solution.py:40
  395.6 42.3 %collective-permute-done.14 = f32[2,2,128,1024]{3,2,1,0:T(8,128)} collective-permute-done((f32[2,2,128,1024]{3,2,1,0:T(8,128)}, f32[2,2,128,1024]{3,2,1,0:T(8,128)}, u32[]{:S(2)}, u32[]{:S(2)}) %collective-permute-start.14) | collective-permute-done | bytes 2097184 | tf_op jit(solution)/shard_map/ppermute | solution.py:40
  441.0 39.8 %product.4.rest_0_ = f32[2,4,1024,1024]{3,2,1,0:T(8,128)} custom-call(f32[2,2,1024,1024]{3,2,1,0:T(8,128)} %all-reduce.2.cloned.1.call-done.left_ref.x_ref, f32[2,2,1024,1024]{3,2,1,0:T(8,128)} %constant_dynamic-update-slice_fusion.18.right_ref), custom_call_target="tpu_custom_call" | custom-call | flops 25769803776 | bytes 83886080 | tf_op jit(solution)/shard_map/product/pallas_call | solution.py:177
  480.8 39.9 %product.5.rest_0_ = f32[2,4,1024,1024]{3,2,1,0:T(8,128)} custom-call(f32[2,2,1024,1024]{3,2,1,0:T(8,128)} %all-reduce.2.cloned.1.call-done.left_ref.x_ref, f32[2,2,1024,1024]{3,2,1,0:T(8,128)} %constant_dynamic-update-slice_fusion.18.right_ref, f32[2,4,1024,1024]{3,2,1,0:T(8,128)} %product.4.rest_0_), custom_call_target="tpu_custom_call", output_to_operand_aliasing={{}: (2, {})} | custom-call | flops 25769803776 | bytes 83886080 | tf_op jit(solution)/shard_map/product/pallas_call | solution.py:177
  522.9 39.9 %product.6.rest_0_ = f32[2,4,1024,1024]{3,2,1,0:T(8,128)} custom-call(f32[2,2,1024,1024]{3,2,1,0:T(8,128)} %all-reduce.2.cloned.1.call-done.left_ref.x_ref, f32[2,2,1024,1024]{3,2,1,0:T(8,128)} %constant_dynamic-update-slice_fusion.26.right_ref, f32[2,4,1024,1024]{3,2,1,0:T(8,128)} %product.5.rest_0_), custom_call_target="tpu_custom_call", output_to_operand_aliasing={{}: (2, {})} | custom-call | flops 25769803776 | bytes 83886080 | tf_op jit(solution)/shard_map/product/pallas_call | solution.py:177
  562.8 39.9 %product.7.rest_0_ = f32[2,4,1024,1024]{3,2,1,0:T(8,128)} custom-call(f32[2,2,1024,1024]{3,2,1,0:T(8,128)} %all-reduce.2.cloned.1.call-done.left_ref.x_ref, f32[2,2,1024,1024]{3,2,1,0:T(8,128)} %constant_dynamic-update-slice_fusion.26.right_ref, f32[2,4,1024,1024]{3,2,1,0:T(8,128)} %product.6.rest_0_), custom_call_target="tpu_custom_call", output_to_operand_aliasing={{}: (2, {})} | custom-call | flops 25769803776 | bytes 83886080 | tf_op jit(solution)/shard_map/product/pallas_call | solution.py:177
  647.8 43.0 %collective-permute-done.17 = f32[2,2,128,1024]{3,2,1,0:T(8,128)} collective-permute-done((f32[2,2,128,1024]{3,2,1,0:T(8,128)}, f32[2,2,128,1024]{3,2,1,0:T(8,128)}, u32[]{:S(2)}, u32[]{:S(2)}) %collective-permute-start.17) | collective-permute-done | bytes 2097184 | tf_op jit(solution)/shard_map/ppermute | solution.py:26
  702.1 71.3 %collective-permute-start.19 = (f32[2,2,128,1024]{3,2,1,0:T(8,128)S(1)}, f32[2,2,128,1024]{3,2,1,0:T(8,128)}, u32[]{:S(2)}, u32[]{:S(2)}) collective-permute-start(f32[2,2,128,1024]{3,2,1,0:T(8,128)S(1)} %get-tuple-element.6), channel_id=1, source_target_pairs={{0,8},{4,12},{8,16},{12,20},{16,24},{20,28},{24,0},{28,4},{1,9},{5... | collective-permute-start | bytes 6291464 | tf_op jit(solution)/shard_map/ppermute | solution.py:42
  782.9 98.1 %collective-permute-start.26 = (f32[2,2,128,1024]{3,2,1,0:T(8,128)S(1)}, f32[2,2,128,1024]{3,2,1,0:T(8,128)}, u32[]{:S(2)}, u32[]{:S(2)}) collective-permute-start(f32[2,2,128,1024]{3,2,1,0:T(8,128)S(1)} %get-tuple-element.7), channel_id=1, source_target_pairs={{0,8},{4,12},{8,16},{12,20},{16,24},{20,28},{24,0},{28,4},{1,9},{5... | collective-permute-start | bytes 6291464 | tf_op jit(solution)/shard_map/ppermute | solution.py:42
  881.0 36.5 %collective-permute-start.21 = (f32[2,2,128,1024]{3,2,1,0:T(8,128)}, f32[2,2,128,1024]{3,2,1,0:T(8,128)}, u32[]{:S(2)}, u32[]{:S(2)}) collective-permute-start(f32[2,2,128,1024]{3,2,1,0:T(8,128)} %collective-permute-done.19), channel_id=1, source_target_pairs={{0,8},{4,12},{8,16},{12,20},{16,24},{20,28},{24,0},{28,4},{1,9},{5... | collective-permute-start | bytes 6291464 | tf_op jit(solution)/shard_map/ppermute | solution.py:42
  927.0 35.5 %collective-permute-start.28 = (f32[2,2,128,1024]{3,2,1,0:T(8,128)}, f32[2,2,128,1024]{3,2,1,0:T(8,128)S(1)}, u32[]{:S(2)}, u32[]{:S(2)}) collective-permute-start(f32[2,2,128,1024]{3,2,1,0:T(8,128)} %collective-permute-done.26), channel_id=1, source_target_pairs={{0,8},{4,12},{8,16},{12,20},{16,24},{20,28},{24,0},{28,4},{1,9},{5... | collective-permute-start | bytes 6291464 | tf_op jit(solution)/shard_map/ppermute | solution.py:42
  1058.5 42.4 %collective-permute-done.20 = f32[2,2,128,1024]{3,2,1,0:T(8,128)} collective-permute-done((f32[2,2,128,1024]{3,2,1,0:T(8,128)}, f32[2,2,128,1024]{3,2,1,0:T(8,128)}, u32[]{:S(2)}, u32[]{:S(2)}) %collective-permute-start.20) | collective-permute-done | bytes 2097184 | tf_op jit(solution)/shard_map/ppermute | solution.py:40
  1150.6 40.3 %collective-permute-done.22 = f32[2,2,128,1024]{3,2,1,0:T(8,128)} collective-permute-done((f32[2,2,128,1024]{3,2,1,0:T(8,128)}, f32[2,2,128,1024]{3,2,1,0:T(8,128)}, u32[]{:S(2)}, u32[]{:S(2)}) %collective-permute-start.22) | collective-permute-done | bytes 2097184 | tf_op jit(solution)/shard_map/ppermute | solution.py:40
  1197.1 38.7 %collective-permute-done.29 = f32[2,2,128,1024]{3,2,1,0:T(8,128)} collective-permute-done((f32[2,2,128,1024]{3,2,1,0:T(8,128)S(1)}, f32[2,2,128,1024]{3,2,1,0:T(8,128)}, u32[]{:S(2)}, u32[]{:S(2)}) %collective-permute-start.29) | collective-permute-done | bytes 2097184 | tf_op jit(solution)/shard_map/ppermute | solution.py:40
  1242.1 38.7 %collective-permute-done.24 = f32[2,2,128,1024]{3,2,1,0:T(8,128)} collective-permute-done((f32[2,2,128,1024]{3,2,1,0:T(8,128)}, f32[2,2,128,1024]{3,2,1,0:T(8,128)}, u32[]{:S(2)}, u32[]{:S(2)}) %collective-permute-start.24) | collective-permute-done | bytes 2097184 | tf_op jit(solution)/shard_map/ppermute | solution.py:40
  1283.9 39.1 %collective-permute-done.31 = f32[2,2,128,1024]{3,2,1,0:T(8,128)S(1)} collective-permute-done((f32[2,2,128,1024]{3,2,1,0:T(8,128)}, f32[2,2,128,1024]{3,2,1,0:T(8,128)S(1)}, u32[]{:S(2)}, u32[]{:S(2)}) %collective-permute-start.31) | collective-permute-done | bytes 2097184 | tf_op jit(solution)/shard_map/ppermute | solution.py:40
  1324.4 44.0 %finish.4.rest_0_ = f32[2,4,1024,1024]{3,2,1,0:T(8,128)} custom-call(f32[2,2,1024,1024]{3,2,1,0:T(8,128)} %bitcast.13, f32[2,2,1024,1024]{3,2,1,0:T(8,128)} %constant_dynamic-update-slice_fusion.right_ref, f32[2,4,1024,1024]{3,2,1,0:T(8,128)} %product.7.rest_0_, f32[2]{0:T(128)S(1)} %dynamic_slice.22.rest_1_, ...), custom_call_target="tpu_custom_call", output_to_operand_aliasing={{}: (2, {})} | custom-call | flops 25769803776 | bytes 83886080 | tf_op jit(solution)/shard_map/finish/pallas_call | solution.py:177
  1368.4 44.0 %finish.5.rest_0_ = f32[2,4,1024,1024]{3,2,1,0:T(8,128)} custom-call(f32[2,2,1024,1024]{3,2,1,0:T(8,128)} %bitcast.14, f32[2,2,1024,1024]{3,2,1,0:T(8,128)} %constant_dynamic-update-slice_fusion.right_ref, f32[2,4,1024,1024]{3,2,1,0:T(8,128)} %finish.4.rest_0_, f32[2]{0:T(128)S(1)} %dynamic_slice.22.rest_1_, ...), custom_call_target="tpu_custom_call", output_to_operand_aliasing={{}: (2, {})} | custom-call | flops 25769803776 | bytes 83886080 | tf_op jit(solution)/shard_map/finish/pallas_call | solution.py:177
  1412.4 44.0 %finish.6.rest_0_ = f32[2,4,1024,1024]{3,2,1,0:T(8,128)} custom-call(f32[2,2,1024,1024]{3,2,1,0:T(8,128)} %bitcast.15, f32[2,2,1024,1024]{3,2,1,0:T(8,128)} %constant_dynamic-update-slice_fusion.8.right_ref, f32[2,4,1024,1024]{3,2,1,0:T(8,128)} %finish.5.rest_0_, f32[2]{0:T(128)S(1)} %dynamic_slice.22.rest_1_, ...), custom_call_target="tpu_custom_call", output_to_operand_aliasing={{}: (2, {})} | custom-call | flops 25769803776 | bytes 83886080 | tf_op jit(solution)/shard_map/finish/pallas_call | solution.py:177
  1456.4 44.0 %finish.7 = f32[2,4,1024,1024]{3,2,1,0:T(8,128)} custom-call(f32[2,2,1024,1024]{3,2,1,0:T(8,128)} %bitcast.16, f32[2,2,1024,1024]{3,2,1,0:T(8,128)} %constant_dynamic-update-slice_fusion.8.right_ref, f32[2,4,1024,1024]{3,2,1,0:T(8,128)} %finish.6.rest_0_, f32[2]{0:T(128)S(1)} %dynamic_slice.22.rest_1_, ...), custom_call_target="tpu_custom_call", output_to_operand_aliasing={{}: (2, {})} | custom-call | flops 25769803776 | bytes 83886080 | tf_op jit(solution)/shard_map/finish/pallas_call | solution.py:177
  (142 shorter events, 387.5 us)
Async XLA Ops:
  6.5 434.5 %all-reduce.2.cloned.1.call-start = ((), (), s32[]{:S(2)}) async-start(), calls=%async_computation | async-start | bytes 33554432 | tf_op jit(solution)/shard_map/psum | solution.py:225
  35.6 1288.8 %all-gather.2.cloned.1.call-start = ((), (), s32[]{:S(2)}) async-start(), calls=%async_computation.1 | async-start | bytes 20971520 | tf_op jit(solution)/shard_map/all_gather | solution.py:248
  115.7 91.7 %collective-permute-start.8 = (f32[2,2,128,1024]{3,2,1,0:T(8,128)}, f32[2,2,128,1024]{3,2,1,0:T(8,128)S(1)}, u32[]{:S(2)}, u32[]{:S(2)}) collective-permute-start(f32[2,2,128,1024]{3,2,1,0:T(8,128)} %get-tuple-element.13), channel_id=1, source_target_pairs={{0,4},{4,0},{8,12},{12,8},{16,20},{20,16},{24,28},{28,24},{1,5},{5... | collective-permute-start | bytes 6291464 | tf_op jit(solution)/shard_map/ppermute | solution.py:40
  117.4 92.0 %collective-permute-start.3 = (f32[2,2,128,1024]{3,2,1,0:T(8,128)S(1)}, f32[2,2,128,1024]{3,2,1,0:T(8,128)S(1)}, u32[]{:S(2)}, u32[]{:S(2)}) collective-permute-start(f32[2,2,128,1024]{3,2,1,0:T(8,128)S(1)} %collective-permute-done.2), channel_id=1, source_target_pairs={{0,4},{4,0},{8,12},{12,8},{16,20},{20,16},{24,28},{28,24},{1,5},{5... | collective-permute-start | bytes 6291464 | tf_op jit(solution)/shard_map/ppermute | solution.py:40
  160.7 123.5 %collective-permute-start.10 = (f32[2,2,128,1024]{3,2,1,0:T(8,128)}, f32[2,2,128,1024]{3,2,1,0:T(8,128)}, u32[]{:S(2)}, u32[]{:S(2)}) collective-permute-start(f32[2,2,128,1024]{3,2,1,0:T(8,128)} %collective-permute-done.9), channel_id=1, source_target_pairs={{0,4},{4,0},{8,12},{12,8},{16,20},{20,16},{24,28},{28,24},{1,5},{5... | collective-permute-start | bytes 6291464 | tf_op jit(solution)/shard_map/ppermute | solution.py:40
  205.6 102.0 %collective-permute-start.5 = (f32[2,2,128,1024]{3,2,1,0:T(8,128)}, f32[2,2,128,1024]{3,2,1,0:T(8,128)}, u32[]{:S(2)}, u32[]{:S(2)}) collective-permute-start(f32[2,2,128,1024]{3,2,1,0:T(8,128)} %collective-permute-done.4), channel_id=1, source_target_pairs={{0,4},{4,0},{8,12},{12,8},{16,20},{20,16},{24,28},{28,24},{1,5},{5... | collective-permute-start | bytes 6291464 | tf_op jit(solution)/shard_map/ppermute | solution.py:40
  207.4 100.4 %collective-permute-start.6 = (f32[2,2,128,1024]{3,2,1,0:T(8,128)}, f32[2,2,128,1024]{3,2,1,0:T(8,128)}, u32[]{:S(2)}, u32[]{:S(2)}) collective-permute-start(f32[2,2,128,1024]{3,2,1,0:T(8,128)} %collective-permute-done.4), channel_id=1, source_target_pairs={{0,8},{4,12},{8,16},{12,20},{16,24},{20,28},{24,0},{28,4},{1,9},{5... | collective-permute-start | bytes 6291464 | tf_op jit(solution)/shard_map/ppermute | solution.py:42
  209.4 179.9 %collective-permute-start.12 = (f32[2,2,128,1024]{3,2,1,0:T(8,128)}, f32[2,2,128,1024]{3,2,1,0:T(8,128)}, u32[]{:S(2)}, u32[]{:S(2)}) collective-permute-start(f32[2,2,128,1024]{3,2,1,0:T(8,128)} %collective-permute-done.11), channel_id=1, source_target_pairs={{0,4},{4,0},{8,12},{12,8},{16,20},{20,16},{24,28},{28,24},{1,5},{5... | collective-permute-start | bytes 6291464 | tf_op jit(solution)/shard_map/ppermute | solution.py:40
  250.6 187.3 %collective-permute-start.14 = (f32[2,2,128,1024]{3,2,1,0:T(8,128)}, f32[2,2,128,1024]{3,2,1,0:T(8,128)}, u32[]{:S(2)}, u32[]{:S(2)}) collective-permute-start(f32[2,2,128,1024]{3,2,1,0:T(8,128)} %collective-permute-done.13), channel_id=1, source_target_pairs={{0,4},{4,0},{8,12},{12,8},{16,20},{20,16},{24,28},{28,24},{1,5},{5... | collective-permute-start | bytes 6291464 | tf_op jit(solution)/shard_map/ppermute | solution.py:40
  284.2 321.0 %collective-permute-start = (f32[2,2,128,1024]{2,3,1,0:T(8,128)}, f32[2,2,128,1024]{2,3,1,0:T(8,128)}, u32[]{:S(2)}, u32[]{:S(2)}) collective-permute-start(f32[2,2,128,1024]{2,3,1,0:T(8,128)} %copy.29), channel_id=1, source_target_pairs={{0,0},{1,8},{2,16},{3,24},{4,4},{5,12},{6,20},{7,28},{8,1},{9,9},{... | collective-permute-start | bytes 6291464 | tf_op jit(solution)/shard_map/ppermute | solution.py:26
  307.6 311.3 %collective-permute-start.15 = (f32[2,2,128,1024]{2,3,1,0:T(8,128)}, f32[2,2,128,1024]{2,3,1,0:T(8,128)}, u32[]{:S(2)}, u32[]{:S(2)}) collective-permute-start(f32[2,2,128,1024]{2,3,1,0:T(8,128)} %copy.30), channel_id=1, source_target_pairs={{0,4},{1,12},{2,20},{3,28},{4,0},{5,8},{6,16},{7,24},{8,5},{9,13},... | collective-permute-start | bytes 6291464 | tf_op jit(solution)/shard_map/ppermute | solution.py:26
  307.8 213.7 %collective-permute-start.7 = (f32[2,2,128,1024]{3,2,1,0:T(8,128)}, f32[2,2,128,1024]{3,2,1,0:T(8,128)S(1)}, u32[]{:S(2)}, u32[]{:S(2)}) collective-permute-start(f32[2,2,128,1024]{3,2,1,0:T(8,128)} %collective-permute-done.6), channel_id=1, source_target_pairs={{0,4},{4,0},{8,12},{12,8},{16,20},{20,16},{24,28},{28,24},{1,5},{5... | collective-permute-start | bytes 6291464 | tf_op jit(solution)/shard_map/ppermute | solution.py:40
  702.1 178.9 %collective-permute-start.19 = (f32[2,2,128,1024]{3,2,1,0:T(8,128)S(1)}, f32[2,2,128,1024]{3,2,1,0:T(8,128)}, u32[]{:S(2)}, u32[]{:S(2)}) collective-permute-start(f32[2,2,128,1024]{3,2,1,0:T(8,128)S(1)} %get-tuple-element.6), channel_id=1, source_target_pairs={{0,8},{4,12},{8,16},{12,20},{16,24},{20,28},{24,0},{28,4},{1,9},{5... | collective-permute-start | bytes 6291464 | tf_op jit(solution)/shard_map/ppermute | solution.py:42
  782.9 144.1 %collective-permute-start.26 = (f32[2,2,128,1024]{3,2,1,0:T(8,128)S(1)}, f32[2,2,128,1024]{3,2,1,0:T(8,128)}, u32[]{:S(2)}, u32[]{:S(2)}) collective-permute-start(f32[2,2,128,1024]{3,2,1,0:T(8,128)S(1)} %get-tuple-element.7), channel_id=1, source_target_pairs={{0,8},{4,12},{8,16},{12,20},{16,24},{20,28},{24,0},{28,4},{1,9},{5... | collective-permute-start | bytes 6291464 | tf_op jit(solution)/shard_map/ppermute | solution.py:42
  881.0 91.1 %collective-permute-start.21 = (f32[2,2,128,1024]{3,2,1,0:T(8,128)}, f32[2,2,128,1024]{3,2,1,0:T(8,128)}, u32[]{:S(2)}, u32[]{:S(2)}) collective-permute-start(f32[2,2,128,1024]{3,2,1,0:T(8,128)} %collective-permute-done.19), channel_id=1, source_target_pairs={{0,8},{4,12},{8,16},{12,20},{16,24},{20,28},{24,0},{28,4},{1,9},{5... | collective-permute-start | bytes 6291464 | tf_op jit(solution)/shard_map/ppermute | solution.py:42
  963.4 92.5 %collective-permute-start.25 = (f32[2,2,128,1024]{3,2,1,0:T(8,128)S(1)}, f32[2,2,128,1024]{3,2,1,0:T(8,128)S(1)}, u32[]{:S(2)}, u32[]{:S(2)}) collective-permute-start(f32[2,2,128,1024]{3,2,1,0:T(8,128)S(1)} %get-tuple-element.7), channel_id=1, source_target_pairs={{0,4},{4,0},{8,12},{12,8},{16,20},{20,16},{24,28},{28,24},{1,5},{5... | collective-permute-start | bytes 6291464 | tf_op jit(solution)/shard_map/ppermute | solution.py:40
  964.5 136.5 %collective-permute-start.20 = (f32[2,2,128,1024]{3,2,1,0:T(8,128)}, f32[2,2,128,1024]{3,2,1,0:T(8,128)}, u32[]{:S(2)}, u32[]{:S(2)}) collective-permute-start(f32[2,2,128,1024]{3,2,1,0:T(8,128)} %collective-permute-done.19), channel_id=1, source_target_pairs={{0,4},{4,0},{8,12},{12,8},{16,20},{20,16},{24,28},{28,24},{1,5},{5... | collective-permute-start | bytes 6291464 | tf_op jit(solution)/shard_map/ppermute | solution.py:40
  972.0 134.5 %collective-permute-start.23 = (f32[2,2,128,1024]{3,2,1,0:T(8,128)}, f32[2,2,128,1024]{3,2,1,0:T(8,128)}, u32[]{:S(2)}, u32[]{:S(2)}) collective-permute-start(f32[2,2,128,1024]{3,2,1,0:T(8,128)} %collective-permute-done.21), channel_id=1, source_target_pairs={{0,8},{4,12},{8,16},{12,20},{16,24},{20,28},{24,0},{28,4},{1,9},{5... | collective-permute-start | bytes 6291464 | tf_op jit(solution)/shard_map/ppermute | solution.py:42
  1017.0 90.9 %collective-permute-start.30 = (f32[2,2,128,1024]{3,2,1,0:T(8,128)S(1)}, f32[2,2,128,1024]{3,2,1,0:T(8,128)}, u32[]{:S(2)}, u32[]{:S(2)}) collective-permute-start(f32[2,2,128,1024]{3,2,1,0:T(8,128)S(1)} %collective-permute-done.28), channel_id=1, source_target_pairs={{0,8},{4,12},{8,16},{12,20},{16,24},{20,28},{24,0},{28,4},{1,9},{5... | collective-permute-start | bytes 6291464 | tf_op jit(solution)/shard_map/ppermute | solution.py:42
  1052.4 93.5 %collective-permute-start.27 = (f32[2,2,128,1024]{3,2,1,0:T(8,128)}, f32[2,2,128,1024]{3,2,1,0:T(8,128)}, u32[]{:S(2)}, u32[]{:S(2)}) collective-permute-start(f32[2,2,128,1024]{3,2,1,0:T(8,128)} %collective-permute-done.26), channel_id=1, source_target_pairs={{0,4},{4,0},{8,12},{12,8},{16,20},{20,16},{24,28},{28,24},{1,5},{5... | collective-permute-start | bytes 6291464 | tf_op jit(solution)/shard_map/ppermute | solution.py:40
  1057.2 133.6 %collective-permute-start.22 = (f32[2,2,128,1024]{3,2,1,0:T(8,128)}, f32[2,2,128,1024]{3,2,1,0:T(8,128)}, u32[]{:S(2)}, u32[]{:S(2)}) collective-permute-start(f32[2,2,128,1024]{3,2,1,0:T(8,128)} %collective-permute-done.21), channel_id=1, source_target_pairs={{0,4},{4,0},{8,12},{12,8},{16,20},{20,16},{24,28},{28,24},{1,5},{5... | collective-permute-start | bytes 6291464 | tf_op jit(solution)/shard_map/ppermute | solution.py:40
  1101.0 134.8 %collective-permute-start.29 = (f32[2,2,128,1024]{3,2,1,0:T(8,128)S(1)}, f32[2,2,128,1024]{3,2,1,0:T(8,128)}, u32[]{:S(2)}, u32[]{:S(2)}) collective-permute-start(f32[2,2,128,1024]{3,2,1,0:T(8,128)S(1)} %collective-permute-done.28), channel_id=1, source_target_pairs={{0,4},{4,0},{8,12},{12,8},{16,20},{20,16},{24,28},{28,24},{1,5},{5... | collective-permute-start | bytes 6291464 | tf_op jit(solution)/shard_map/ppermute | solution.py:40
  1106.5 174.2 %collective-permute-start.24 = (f32[2,2,128,1024]{3,2,1,0:T(8,128)}, f32[2,2,128,1024]{3,2,1,0:T(8,128)}, u32[]{:S(2)}, u32[]{:S(2)}) collective-permute-start(f32[2,2,128,1024]{3,2,1,0:T(8,128)} %collective-permute-done.23), channel_id=1, source_target_pairs={{0,4},{4,0},{8,12},{12,8},{16,20},{20,16},{24,28},{28,24},{1,5},{5... | collective-permute-start | bytes 6291464 | tf_op jit(solution)/shard_map/ppermute | solution.py:40
  1107.9 215.1 %collective-permute-start.31 = (f32[2,2,128,1024]{3,2,1,0:T(8,128)}, f32[2,2,128,1024]{3,2,1,0:T(8,128)S(1)}, u32[]{:S(2)}, u32[]{:S(2)}) collective-permute-start(f32[2,2,128,1024]{3,2,1,0:T(8,128)} %collective-permute-done.30), channel_id=1, source_target_pairs={{0,4},{4,0},{8,12},{12,8},{16,20},{20,16},{24,28},{28,24},{1,5},{5... | collective-permute-start | bytes 6291464 | tf_op jit(solution)/shard_map/ppermute | solution.py:40
  (25 other events, 3343.4 us)
Sparse Core Ops, SparseCore 0:
  35.7 311.7 all-reduce.1
  629.4 165.8 all-gather.1
